TPU v7x, 128 devices: a whole 4x4x4 slice. The times are simulated.
128 devices in a mesh: year: 4 (over z_lo, core), tile: 32 (over x, z_hi, y).
Axes of the slice: x: 4, y: 4, z: 4 (z_hi: 2, z_lo: 2; z = z_hi * 2 + z_lo), core: 2. Of those that a mesh axis runs over, the one named last changes fastest.
Arguments:
- station_tile: int32 [131072, 1], P(('year', 'tile')), may hold values from 0 to 31; in each aligned block of 1024 rows (0 to 1023, 1024 to 2047, ...) at most 96 rows name the same one
- station_cell: int32 [131072], P(('year', 'tile')), may hold values from 0 to 262143
- station_value: float32 [131072], P(('year', 'tile')), may hold values from -6 to 6
- class_ids: int32 [128, 8192], P(None, 'tile'), may hold values from 0 to 15
- coeff_table: float32 [3, 16], replicated, may hold values from 0.2 to 2
- lag_blocks: float32 [5, 128, 128], replicated, may hold values from -0.5 to 0.5
Outputs:
- filtered: float32 [32, 128, 8192], P('year', None, 'tile')
Inputs may be any that keep to these rules, and one draw needn't show every extreme that they name: `station_tile`: in the rows of one device no tile is named by more than 96 rows, a bound that some block reaches.
All inputs are finite; a program needn't handle non-finite values.
Results may differ from a plain program's by a relative error of at most 0.00013.
Values sent between devices are 32-bit elements; how exact they have to be, the bound alone decides.
A program may use at most 192 MiB of HBM per device.

v0:
```python
import jax
import jax.numpy as jnp
from jax import lax
from jax.experimental import pallas as pl
from jax.experimental.pallas import tpu as pltpu
from jax.sharding import PartitionSpec as P

DAY_DEV = 8
LAT = 128
LON_DEV = 256
CAP = 96
LANES = 128
NTILE = 32
NYEAR = 4
NCLASS = 16
GROUPS = ((0, 8), (8, 8), (16, 8), (24, 8))
FAR_PARTS = ((0, 16), (16, 16))
MOST = 16
LAGS = 5
HALO = 2
DAYS_EXT = DAY_DEV + 2 * HALO
PAD = 8
F32 = jnp.float32
BF16 = jnp.bfloat16


def dot_nt(a, b):
    return lax.dot_general(a, b, (((1,), (1,)), ((), ())), preferred_element_type=F32)


def split2(x):
    hi = x.astype(BF16).astype(F32)
    return hi, x - hi


def hot(mask):
    return jnp.where(mask, 1.0, 0.0).astype(BF16)


def hops(offset):
    return sum(min(o, n - o) * step for o, n, step in zip(offset, (4, 2, 4), (1, 2, 1)))


OFFSETS = sorted(((x, z, y) for x in range(4) for z in range(2) for y in range(4)), key=hops)


def bucket(tile, cell, value, pieces_ref, slots_ref, send_ref):
    hi, mid = split2(value)
    day = jnp.right_shift(cell, 15).astype(F32)
    row = jnp.bitwise_and(jnp.right_shift(cell, 8), 127).astype(F32)
    col = jnp.bitwise_and(cell, 255).astype(F32)
    of_tile = lax.broadcasted_iota(jnp.int32, (NTILE, LANES), 0)
    masks = [tile[b : b + 1, :] == of_tile for b in range(8)]
    ones = jnp.concatenate([hot(m) for m in masks], axis=0)
    source = lax.broadcasted_iota(jnp.int32, (LANES, 2 * LANES), 0)
    target = lax.broadcasted_iota(jnp.int32, (LANES, 2 * LANES), 1)
    before = hot((source < target) | (target >= LANES))
    counts = jnp.dot(ones, before, preferred_element_type=F32)
    base = jnp.zeros((NTILE, LANES), F32)
    slot_iota = lax.broadcasted_iota(jnp.int32, (LANES, LANES), 0).astype(F32)
    for b in range(8):
        lanes = slice(b * LANES, (b + 1) * LANES)
        rank = counts[b * NTILE : (b + 1) * NTILE, :LANES] + base
        base = base + counts[b * NTILE : (b + 1) * NTILE, LANES:]
        slot = jnp.sum(jnp.where(masks[b], rank, 0.0), axis=0, keepdims=True)
        slots_ref[:, lanes] = hot(slot_iota == slot)
        for q, piece in enumerate((hi, mid, day, row, col)):
            pieces_ref[q * NTILE : (q + 1) * NTILE, lanes] = jnp.where(
                masks[b], piece[b : b + 1, :], 0.0
            ).astype(BF16)
    out = dot_nt(pieces_ref[...], slots_ref[...])
    part = [out[q * NTILE : (q + 1) * NTILE] for q in range(5)]
    values = part[0] + part[1]
    cells = part[2] * 32768.0 + part[3] * 256.0 + part[4]
    for q, x in enumerate((values, cells)):
        send_ref[1 : NTILE + 1, q, :] = x
        send_ref[0:1, q, :] = x[NTILE - 1 :]
        send_ref[NTILE + 1 : NTILE + 2, q, :] = x[:1]


def dense(lists):
    lane = lax.broadcasted_iota(jnp.int32, (1, LANES), 1)
    turned = [pltpu.roll(lists, shift, 1) for shift in (96, 64, 32)]
    return [
        jnp.where(lane < CAP, lists[i + j : i + j + 1], turned[j][i + 3 : i + 4])
        for i in range(0, lists.shape[0], 4)
        for j in range(3)
    ]


def entries(recv_ref, senders, which):
    at = slice(senders[0], sum(senders))
    hi, lo = split2(recv_ref[at, which, 0, :])
    return hi, lo, recv_ref[at, which, 1, :].astype(jnp.int32)


def scatter(recv_ref, senders, days, lhs_ref, rhs_ref, field, first):
    hi, lo, cell = entries(recv_ref, senders, 1)
    hi, lo = dense(hi), dense(lo)
    col = dense(jnp.bitwise_and(cell, 255))
    plane = dense(jnp.right_shift(cell, 8))
    depth = len(col) * LANES
    column = lax.broadcasted_iota(jnp.int32, (LON_DEV, LANES), 0)
    latitude = lax.broadcasted_iota(jnp.int32, (LAT, LANES), 0)
    for k in range(len(col)):
        lanes = slice(k * LANES, (k + 1) * LANES)
        here = col[k] == column
        lhs_ref[:LON_DEV, lanes] = jnp.where(here, hi[k], 0.0).astype(BF16)
        lhs_ref[LON_DEV:, lanes] = jnp.where(here, lo[k], 0.0).astype(BF16)
    for i, d in enumerate(days):
        for k in range(len(col)):
            rhs_ref[i * LAT : (i + 1) * LAT, k * LANES : (k + 1) * LANES] = hot(
                plane[k] - d * LAT == latitude
            )
    for pair in range(len(days) // 2):
        both = dot_nt(
            lhs_ref[:, :depth], rhs_ref[2 * LAT * pair : 2 * LAT * (pair + 1), :depth]
        )
        both = both[:LON_DEV] + both[LON_DEV:]
        for i in range(2):
            part = both[:, i * LAT : (i + 1) * LAT]
            e = first + 2 * pair + i
            if senders[0] == 0:
                field[e, PAD : PAD + LON_DEV] = part
            else:
                field[e, PAD : PAD + LON_DEV] += part


def scatter_edges(recv_ref, senders, count, number_of, lhs_ref, rhs_ref, edges, first):
    rows = 4 * count
    latitude = lax.broadcasted_iota(jnp.int32, (LAT, LANES), 0)
    number = lax.broadcasted_iota(jnp.int32, (rows, LANES), 0)
    blocks = 3 * senders[1] // 4
    for j, which in enumerate((0, 2)):
        hi, lo, cell = entries(recv_ref, senders, which)
        col = jnp.bitwise_and(cell, 255)
        near = col >= LON_DEV - 2 if which == 0 else col < 2
        place = 4 * number_of(jnp.right_shift(cell, 15)) + (
            col - (LON_DEV - 2) if which == 0 else col + 2
        )
        place = dense(jnp.where(near, place, -1))
        lat = dense(jnp.bitwise_and(jnp.right_shift(cell, 8), LAT - 1))
        hi, lo = dense(hi), dense(lo)
        for k in range(blocks):
            lanes = slice((blocks * j + k) * LANES, (blocks * j + k + 1) * LANES)
            here = place[k] == number
            lhs_ref[:rows, lanes] = jnp.where(here, hi[k], 0.0).astype(BF16)
            lhs_ref[rows : 2 * rows, lanes] = jnp.where(here, lo[k], 0.0).astype(BF16)
            rhs_ref[:, lanes] = hot(lat[k] == latitude)
    depth = 2 * blocks * LANES
    both = dot_nt(lhs_ref[: 2 * rows, :depth], rhs_ref[:, :depth])
    both = both[:rows] + both[rows:]
    for i in range(count):
        if senders[0] == 0:
            edges[first + i] = both[4 * i : 4 * i + 4]
        else:
            edges[first + i] += both[4 * i : 4 * i + 4]


def kernel(
    tile_hbm,
    cell_hbm,
    value_hbm,
    class_hbm,
    coeff_hbm,
    lag_hbm,
    out_ref,
    tile_ref,
    cell_ref,
    value_ref,
    class_ref,
    coeff_ref,
    lag_ref,
    pieces_ref,
    slots_ref,
    send_ref,
    recv_own,
    recv_far,
    class_t,
    class_halo,
    coef_ref,
    lhs_ref,
    rhs_ref,
    edge_lhs,
    edge_rhs,
    field,
    edges,
    once,
    mix_ref,
    smooth_hi,
    smooth_lo,
    near_out,
    near_in,
    load_sem,
    list_send,
    list_recv,
    far_send,
    far_recv,
    near_send,
    near_recv,
    class_send,
    class_recv,
):
    loads = [
        pltpu.make_async_copy(source, target, load_sem.at[i])
        for i, (source, target) in enumerate(
            (
                (tile_hbm, tile_ref),
                (cell_hbm, cell_ref),
                (value_hbm, value_ref),
                (class_hbm, class_ref),
                (coeff_hbm, coeff_ref),
                (lag_hbm, lag_ref),
            )
        )
    ]
    for load in loads[:3]:
        load.start()

    segment = lax.axis_index("year")
    me = lax.axis_index("tile")
    odd = lax.rem(segment, 2)
    near = segment + 1 - 2 * odd
    far = lax.rem(segment + NYEAR - 1 + 2 * odd, NYEAR)

    def day_of(d):
        return d + odd * (DAY_DEV - 1 - 2 * d)

    east = lax.rem(me + 1, NTILE)
    west = lax.rem(me + NTILE - 1, NTILE)
    x, z, y = me // 8, lax.rem(me // 4, 2), lax.rem(me, 4)
    peers = [
        lax.rem(x + dx, 4) * 8 + lax.rem(z + dz, 2) * 4 + lax.rem(y + dy, 4)
        for dx, dz, dy in OFFSETS
    ]

    barrier = pltpu.get_barrier_semaphore()
    for i in reversed(range(1, NTILE)):
        pl.semaphore_signal(barrier, inc=1, device_id={"tile": peers[i]})
    pl.semaphore_signal(barrier, inc=1, device_id={"year": near})
    pl.semaphore_signal(barrier, inc=1, device_id={"year": far})
    for load in loads[3:]:
        load.start()

    for load in loads[:3]:
        load.wait()
    bucket(tile_ref[...], cell_ref[...], value_ref[...], pieces_ref, slots_ref, send_ref)

    pl.semaphore_wait(barrier, NTILE + 1)

    for g, (low, count) in reversed(list(enumerate(GROUPS))):
        for i in reversed(range(max(low, 1), low + count)):
            pltpu.make_async_remote_copy(
                send_ref.at[pl.ds(peers[i], 3)],
                recv_own.at[i],
                list_send,
                list_recv.at[g],
                device_id={"tile": peers[i]},
            ).start()
    recv_own[0] = send_ref[pl.ds(me, 3)]
    loads[3].wait()
    class_t[...] = jnp.transpose(class_ref[...])
    class_copies = [
        pltpu.make_async_remote_copy(
            class_t.at[pl.ds(start, PAD)],
            class_halo.at[1 - side],
            class_send.at[side],
            class_recv.at[1 - side],
            device_id={"tile": tgt},
        )
        for side, start, tgt in ((0, 0, west), (1, LON_DEV - PAD, east))
    ]
    for copy in class_copies:
        copy.start()

    loads[4].wait()
    loads[5].wait()
    mix_ref[...] = jnp.zeros_like(mix_ref)
    for k in range(LAGS):
        hi, lo = split2(lag_ref[k + odd * (LAGS - 1 - 2 * k)])
        for i in range(2):
            lanes = slice((k + i) * LAT, (k + i + 1) * LAT)
            mix_ref[i * LAT : (i + 1) * LAT, lanes] = hi.astype(BF16)
            mix_ref[(2 + i) * LAT : (3 + i) * LAT, lanes] = lo.astype(BF16)

    def coefficients(ids, rows):
        kappa = hzon = hmer = jnp.zeros(ids.shape, F32)
        for c in range(NCLASS):
            here = ids == c
            kappa = jnp.where(here, coeff_ref[0, c], kappa)
            hzon = jnp.where(here, coeff_ref[1, c], hzon)
            hmer = jnp.where(here, coeff_ref[2, c], hmer)
        lane = lax.broadcasted_iota(jnp.int32, ids.shape, 1)
        coef_ref[0, rows] = kappa + 2.0 * hzon + 2.0 * hmer
        coef_ref[1, rows] = hzon
        coef_ref[2, rows] = jnp.where(lane < LAT - 1, hmer, 0.0)
        coef_ref[3, rows] = jnp.where(lane > 0, hmer, 0.0)

    coefficients(class_t[...], slice(PAD, PAD + LON_DEV))

    forwarded = []

    def own(group):
        start, count = GROUPS[group]
        low = max(1, start)
        pltpu.make_async_remote_copy(
            recv_own.at[pl.ds(low, start + count - low)],
            recv_own.at[pl.ds(low, start + count - low)],
            list_send,
            list_recv.at[group],
            device_id={"tile": east},
        ).wait_recv()
        copy = pltpu.make_async_remote_copy(
            recv_own.at[pl.ds(start, count)],
            recv_far.at[pl.ds(start, count)],
            far_send.at[group],
            far_recv.at[group],
            device_id={"year": far},
        )
        copy.start()
        forwarded.append(copy)
        days = [day_of(d) for d in range(DAY_DEV)]
        scatter(recv_own, GROUPS[group], days, lhs_ref, rhs_ref, field, HALO)
        scatter_edges(
            recv_own, GROUPS[group], DAY_DEV, day_of, edge_lhs, edge_rhs, edges, HALO
        )

    def halo(part):
        senders = FAR_PARTS[part]
        for group, (start, _) in enumerate(GROUPS):
            if senders[0] <= start < sum(senders):
                forwarded[group].wait_recv()
        days = [day_of(d + DAY_DEV - HALO) for d in range(HALO)]
        scatter(recv_far, senders, days, lhs_ref, rhs_ref, field, 0)
        scatter_edges(
            recv_far,
            senders,
            HALO,
            lambda day: day_of(day) - (DAY_DEV - HALO),
            edge_lhs,
            edge_rhs,
            edges,
            0,
        )

    def stencil(src, at, rows):
        v = src[at + (rows,)]
        e = src[at + (slice(rows.start + 1, rows.stop + 1),)]
        w = src[at + (slice(rows.start - 1, rows.stop - 1),)]
        north = pltpu.roll(v, LAT - 1, 1)
        south = pltpu.roll(v, 1, 1)
        return (
            coef_ref[0, rows] * v
            - coef_ref[1, rows] * (e + w)
            - coef_ref[2, rows] * north
            - coef_ref[3, rows] * south
        )

    def keep(e, plane):
        hi, lo = split2(plane)
        smooth_hi[e] = hi.astype(BF16)
        smooth_lo[e] = lo.astype(BF16)

    def smooth(e):
        field[e, PAD - 2 : PAD] = edges[e, :2]
        field[e, PAD + LON_DEV : PAD + LON_DEV + 2] = edges[e, 2:]
        for rows in (
            slice(PAD, PAD + LON_DEV),
            slice(PAD - 1, PAD),
            slice(PAD + LON_DEV, PAD + LON_DEV + 1),
        ):
            once[rows] = stencil(field, (e,), rows)
        twice = stencil(once, (), slice(PAD, PAD + LON_DEV))
        keep(e, twice)
        return twice

    def mix(pair):
        window = range(2 * pair, 2 * pair + LAGS + 1)
        hi = jnp.concatenate([smooth_hi[e] for e in window], axis=1)
        lo = jnp.concatenate([smooth_lo[e] for e in window], axis=1)
        first = dot_nt(mix_ref[...], hi)
        second = dot_nt(mix_ref[: 2 * LAT], lo)
        mixed = first[: 2 * LAT] + (first[2 * LAT :] + second)
        out_ref[day_of(2 * pair)] = mixed[:LAT]
        out_ref[day_of(2 * pair + 1)] = mixed[LAT:]

    own(0)
    own(1)
    for copy in class_copies:
        copy.wait()
    coefficients(class_halo[0], slice(0, PAD))
    coefficients(class_halo[1], slice(PAD + LON_DEV, 2 * PAD + LON_DEV))
    own(2)
    halo(0)
    own(3)
    near_copies = []
    for i, e in enumerate((HALO + DAY_DEV - 1, HALO + DAY_DEV - 2)):
        near_out[i] = smooth(e)
        copy = pltpu.make_async_remote_copy(
            near_out.at[i], near_in.at[i], near_send.at[i], near_recv.at[i], device_id={"year": near}
        )
        copy.start()
        near_copies.append(copy)
    for d in range(DAY_DEV - 2):
        smooth(HALO + d)
    mix(1)
    mix(2)
    for i, copy in enumerate(near_copies):
        copy.wait()
        keep(HALO + DAY_DEV + i, near_in[i])
    mix(3)
    halo(1)
    smooth(1)
    smooth(0)
    mix(0)

    pltpu.make_async_remote_copy(
        recv_own.at[pl.ds(1, NTILE - 1)],
        recv_own.at[pl.ds(1, NTILE - 1)],
        list_send,
        list_recv.at[0],
        device_id={"tile": east},
    ).wait_send()
    for copy in forwarded:
        copy.wait_send()


def body(station_tile, station_cell, station_value, class_ids, coeff_table, lag_blocks):
    hbm = pl.BlockSpec(memory_space=pltpu.HBM)
    dma = pltpu.SemaphoreType.DMA
    groups = len(GROUPS)
    return pl.pallas_call(
        kernel,
        out_shape=pltpu.VMEM((DAY_DEV, LAT, LON_DEV), F32),
        in_specs=[hbm] * 6,
        out_specs=pl.BlockSpec(memory_space=pltpu.VMEM),
        scratch_shapes=[
            pltpu.VMEM((8, LANES), jnp.int32),
            pltpu.VMEM((8, LANES), jnp.int32),
            pltpu.VMEM((8, LANES), F32),
            pltpu.VMEM((LAT, LON_DEV), jnp.int32),
            pltpu.SMEM((3, NCLASS), F32),
            pltpu.VMEM((LAGS, LAT, LAT), F32),
            pltpu.VMEM((5 * NTILE, 8 * LANES), BF16),
            pltpu.VMEM((LANES, 8 * LANES), BF16),
            pltpu.VMEM((NTILE + 2, 2, LANES), F32),
            pltpu.VMEM((NTILE, 3, 2, LANES), F32),
            pltpu.VMEM((NTILE, 3, 2, LANES), F32),
            pltpu.VMEM((LON_DEV, LAT), jnp.int32),
            pltpu.VMEM((2, PAD, LAT), jnp.int32),
            pltpu.VMEM((4, LON_DEV + 2 * PAD, LAT), F32),
            pltpu.VMEM((2 * LON_DEV, MOST * CAP), BF16),
            pltpu.VMEM((DAY_DEV * LAT, MOST * CAP), BF16),
            pltpu.VMEM((8 * DAY_DEV, 2 * MOST * CAP), BF16),
            pltpu.VMEM((LAT, 2 * MOST * CAP), BF16),
            pltpu.VMEM((DAYS_EXT, LON_DEV + 2 * PAD, LAT), F32),
            pltpu.VMEM((DAYS_EXT, 4, LAT), F32),
            pltpu.VMEM((LON_DEV + 2 * PAD, LAT), F32),
            pltpu.VMEM((4 * LAT, (LAGS + 1) * LAT), BF16),
            pltpu.VMEM((DAYS_EXT, LON_DEV, LAT), BF16),
            pltpu.VMEM((DAYS_EXT, LON_DEV, LAT), BF16),
            pltpu.VMEM((HALO, LON_DEV, LAT), F32),
            pltpu.VMEM((HALO, LON_DEV, LAT), F32),
            dma((6,)),
            dma,
            dma((groups,)),
            dma((groups,)),
            dma((groups,)),
            dma((HALO,)),
            dma((HALO,)),
            dma((2,)),
            dma((2,)),
        ],
        compiler_params=pltpu.CompilerParams(
            collective_id=0, has_side_effects=True, vmem_limit_bytes=40 * 2**20
        ),
    )(
        *(
            pltpu.with_memory_space_constraint(x, pltpu.HBM)
            for x in (
                station_tile.reshape(8, LANES),
                station_cell.reshape(8, LANES),
                station_value.reshape(8, LANES),
                class_ids,
                coeff_table,
                lag_blocks,
            )
        )
    )


def solution(mesh):
    in_specs = (
        P(("year", "tile"), None),
        P(("year", "tile")),
        P(("year", "tile")),
        P(None, "tile"),
        P(),
        P(),
    )
    out_specs = P("year", None, "tile")
    return jax.shard_map(body, mesh=mesh, in_specs=in_specs, out_specs=out_specs, check_vma=False)
```

profile of v0, /device:TPU:1, one launch (start us, length us, event | category | flops | bytes accessed | tf_op | source)
XLA Modules:
  0.0 28.3 jit_solution(8478640934996345652)
XLA Ops:
  0.0 27.3 %shard_map.64 = f32[8,128,256]{2,1,0:T(8,128)S(1)} custom-call(s32[8,128]{1,0:T(8,128)} %bitcast.3, s32[8,128]{1,0:T(8,128)} %bitcast.4, f32[8,128]{1,0:T(8,128)} %bitcast.5, s32[128,256]{1,0:T(8,128)} %class_hbm.1, f32[3,16]{1,0:T(4,128)} %coeff_hbm.1, f32[5,128,128]{2,1,0:T(8,128)} %lag_hbm.1), custom_call_target="tpu_custom_call" | custom-call | tf_op jit(solution)/shard_map/pallas_call | solution.py:432
  27.3 1.0 %copy.8 = f32[8,128,256]{2,1,0:T(8,128)} copy(f32[8,128,256]{2,1,0:T(8,128)S(1)} %shard_map.64) | data formatting | bytes 2097152
where the time goes:
time: 28.4 us; the launch traced here: 28.3 us
  Pallas kernels  27.3 us (96%)
  local copies, waits for them, and re-layouts  0.97 us (3%)
    pallas_call x1, Pallas kernels, body(): pl.pallas_call(kernel, out_shape=pltpu.VMEM((DAY_DEV, LAT, LON_DEV), F32)...  27.3 us
    unnamed x1, local copies, waits for them, and re-layouts  0.97 us

commit v1 on v0

--- a/solution.py
+++ b/solution.py
@@ -13,9 +13,9 @@
 NTILE = 32
 NYEAR = 4
 NCLASS = 16
-GROUPS = ((0, 8), (8, 8), (16, 8), (24, 8))
-FAR_PARTS = ((0, 16), (16, 16))
-MOST = 16
+GROUPS = ((0, 16), (16, 16))
+FAR_PARTS = ((0, 32),)
+MOST = 32
 LAGS = 5
 HALO = 2
 DAYS_EXT = DAY_DEV + 2 * HALO
@@ -42,6 +42,21 @@
 
 
 OFFSETS = sorted(((x, z, y) for x in range(4) for z in range(2) for y in range(4)), key=hops)
+
+
+def spread(row, count):
+    few = jnp.broadcast_to(row.astype(F32), (16, LANES)).astype(BF16)
+    return jnp.concatenate([few] * (count // 16), axis=0)
+
+
+def numbers(count):
+    return lax.broadcasted_iota(jnp.int32, (count, LANES), 0).astype(F32).astype(BF16)
+
+
+def pick(row, iota, piece=None):
+    count = iota.shape[0]
+    value = jnp.ones((), BF16) if piece is None else spread(piece, count)
+    return jnp.where(spread(row, count) == iota, value, jnp.zeros((), BF16))
 
 
 def bucket(tile, cell, value, pieces_ref, slots_ref, send_ref):
@@ -90,8 +105,12 @@
 
 def entries(recv_ref, senders, which):
     at = slice(senders[0], sum(senders))
-    hi, lo = split2(recv_ref[at, which, 0, :])
-    return hi, lo, recv_ref[at, which, 1, :].astype(jnp.int32)
+    if len(recv_ref.shape) == 3:
+        value, cell = recv_ref[at, 0, :], recv_ref[at, 1, :]
+    else:
+        value, cell = recv_ref[at, which, 0, :], recv_ref[at, which, 1, :]
+    hi, lo = split2(value)
+    return hi, lo, cell.astype(jnp.int32)
 
 
 def scatter(recv_ref, senders, days, lhs_ref, rhs_ref, field, first):
@@ -100,17 +119,15 @@
     col = dense(jnp.bitwise_and(cell, 255))
     plane = dense(jnp.right_shift(cell, 8))
     depth = len(col) * LANES
-    column = lax.broadcasted_iota(jnp.int32, (LON_DEV, LANES), 0)
-    latitude = lax.broadcasted_iota(jnp.int32, (LAT, LANES), 0)
+    column, latitude = numbers(LON_DEV), numbers(LAT)
     for k in range(len(col)):
         lanes = slice(k * LANES, (k + 1) * LANES)
-        here = col[k] == column
-        lhs_ref[:LON_DEV, lanes] = jnp.where(here, hi[k], 0.0).astype(BF16)
-        lhs_ref[LON_DEV:, lanes] = jnp.where(here, lo[k], 0.0).astype(BF16)
+        lhs_ref[:LON_DEV, lanes] = pick(col[k], column, hi[k])
+        lhs_ref[LON_DEV:, lanes] = pick(col[k], column, lo[k])
     for i, d in enumerate(days):
         for k in range(len(col)):
-            rhs_ref[i * LAT : (i + 1) * LAT, k * LANES : (k + 1) * LANES] = hot(
-                plane[k] - d * LAT == latitude
+            rhs_ref[i * LAT : (i + 1) * LAT, k * LANES : (k + 1) * LANES] = pick(
+                plane[k] - d * LAT, latitude
             )
     for pair in range(len(days) // 2):
         both = dot_nt(
@@ -128,8 +145,8 @@
 
 def scatter_edges(recv_ref, senders, count, number_of, lhs_ref, rhs_ref, edges, first):
     rows = 4 * count
-    latitude = lax.broadcasted_iota(jnp.int32, (LAT, LANES), 0)
-    number = lax.broadcasted_iota(jnp.int32, (rows, LANES), 0)
+    padded = max(rows, 16)
+    latitude, number = numbers(LAT), numbers(padded)
     blocks = 3 * senders[1] // 4
     for j, which in enumerate((0, 2)):
         hi, lo, cell = entries(recv_ref, senders, which)
@@ -143,13 +160,12 @@
         hi, lo = dense(hi), dense(lo)
         for k in range(blocks):
             lanes = slice((blocks * j + k) * LANES, (blocks * j + k + 1) * LANES)
-            here = place[k] == number
-            lhs_ref[:rows, lanes] = jnp.where(here, hi[k], 0.0).astype(BF16)
-            lhs_ref[rows : 2 * rows, lanes] = jnp.where(here, lo[k], 0.0).astype(BF16)
-            rhs_ref[:, lanes] = hot(lat[k] == latitude)
+            lhs_ref[:padded, lanes] = pick(place[k], number, hi[k])
+            lhs_ref[padded : 2 * padded, lanes] = pick(place[k], number, lo[k])
+            rhs_ref[:, lanes] = pick(lat[k], latitude)
     depth = 2 * blocks * LANES
-    both = dot_nt(lhs_ref[: 2 * rows, :depth], rhs_ref[:, :depth])
-    both = both[:rows] + both[rows:]
+    both = dot_nt(lhs_ref[: 2 * padded, :depth], rhs_ref[:, :depth])
+    both = both[:padded] + both[padded:]
     for i in range(count):
         if senders[0] == 0:
             edges[first + i] = both[4 * i : 4 * i + 4]
@@ -198,6 +214,8 @@
     far_recv,
     near_send,
     near_recv,
+    edge_send,
+    edge_recv,
     class_send,
     class_recv,
 ):
@@ -299,6 +317,16 @@
     coefficients(class_t[...], slice(PAD, PAD + LON_DEV))
 
     forwarded = []
+    edge_copies = [
+        pltpu.make_async_remote_copy(
+            edges.at[HALO + i],
+            edges.at[HALO - 1 - i],
+            edge_send.at[i],
+            edge_recv.at[HALO - 1 - i],
+            device_id={"year": far},
+        )
+        for i in range(HALO)
+    ]
 
     def own(group):
         start, count = GROUPS[group]
@@ -311,7 +339,7 @@
             device_id={"tile": east},
         ).wait_recv()
         copy = pltpu.make_async_remote_copy(
-            recv_own.at[pl.ds(start, count)],
+            recv_own.at[pl.ds(start, count), 1],
             recv_far.at[pl.ds(start, count)],
             far_send.at[group],
             far_recv.at[group],
@@ -320,10 +348,13 @@
         copy.start()
         forwarded.append(copy)
         days = [day_of(d) for d in range(DAY_DEV)]
-        scatter(recv_own, GROUPS[group], days, lhs_ref, rhs_ref, field, HALO)
         scatter_edges(
             recv_own, GROUPS[group], DAY_DEV, day_of, edge_lhs, edge_rhs, edges, HALO
         )
+        if group == len(GROUPS) - 1:
+            for copy in edge_copies:
+                copy.start()
+        scatter(recv_own, GROUPS[group], days, lhs_ref, rhs_ref, field, HALO)
 
     def halo(part):
         senders = FAR_PARTS[part]
@@ -332,16 +363,6 @@
                 forwarded[group].wait_recv()
         days = [day_of(d + DAY_DEV - HALO) for d in range(HALO)]
         scatter(recv_far, senders, days, lhs_ref, rhs_ref, field, 0)
-        scatter_edges(
-            recv_far,
-            senders,
-            HALO,
-            lambda day: day_of(day) - (DAY_DEV - HALO),
-            edge_lhs,
-            edge_rhs,
-            edges,
-            0,
-        )
 
     def stencil(src, at, rows):
         v = src[at + (rows,)]
@@ -384,15 +405,12 @@
         out_ref[day_of(2 * pair)] = mixed[:LAT]
         out_ref[day_of(2 * pair + 1)] = mixed[LAT:]
 
-    own(0)
-    own(1)
     for copy in class_copies:
         copy.wait()
     coefficients(class_halo[0], slice(0, PAD))
     coefficients(class_halo[1], slice(PAD + LON_DEV, 2 * PAD + LON_DEV))
-    own(2)
-    halo(0)
-    own(3)
+    for group in range(len(GROUPS)):
+        own(group)
     near_copies = []
     for i, e in enumerate((HALO + DAY_DEV - 1, HALO + DAY_DEV - 2)):
         near_out[i] = smooth(e)
@@ -409,7 +427,10 @@
         copy.wait()
         keep(HALO + DAY_DEV + i, near_in[i])
     mix(3)
-    halo(1)
+    for part in range(len(FAR_PARTS)):
+        halo(part)
+    for copy in edge_copies:
+        copy.wait()
     smooth(1)
     smooth(0)
     mix(0)
@@ -445,7 +466,7 @@
             pltpu.VMEM((LANES, 8 * LANES), BF16),
             pltpu.VMEM((NTILE + 2, 2, LANES), F32),
             pltpu.VMEM((NTILE, 3, 2, LANES), F32),
-            pltpu.VMEM((NTILE, 3, 2, LANES), F32),
+            pltpu.VMEM((NTILE, 2, LANES), F32),
             pltpu.VMEM((LON_DEV, LAT), jnp.int32),
             pltpu.VMEM((2, PAD, LAT), jnp.int32),
             pltpu.VMEM((4, LON_DEV + 2 * PAD, LAT), F32),
@@ -468,6 +489,8 @@
             dma((groups,)),
             dma((HALO,)),
             dma((HALO,)),
+            dma((HALO,)),
+            dma((HALO,)),
             dma((2,)),
             dma((2,)),
         ],

time: 28.4 us -> 26.2 us (0.923)
  Pallas kernels: 27.3 us -> 25.1 us
    pallas_call x1, Pallas kernels: 27.3 us -> 25.1 us  [body(): pl.pallas_call(kernel, out_shape=pltpu.VMEM((DAY_DEV, LAT, LON_DEV), F32)...]
where the time goes in v1:
time: 26.2 us; the launch traced here: 26.1 us
  Pallas kernels  25.1 us (96%)
  local copies, waits for them, and re-layouts  0.97 us (4%)
    pallas_call x1, Pallas kernels, body(): pl.pallas_call(kernel, out_shape=pltpu.VMEM((DAY_DEV, LAT, LON_DEV), F32)...  25.1 us
    unnamed x1, local copies, waits for them, and re-layouts  0.97 us

profile of v1, /device:TPU:1, one launch (start us, length us, event | category | flops | bytes accessed | tf_op | source)
XLA Modules:
  0.0 26.1 jit_solution(2051057114036299632)
XLA Ops:
  0.0 25.1 %shard_map.64 = f32[8,128,256]{2,1,0:T(8,128)S(1)} custom-call(s32[8,128]{1,0:T(8,128)} %bitcast.3, s32[8,128]{1,0:T(8,128)} %bitcast.4, f32[8,128]{1,0:T(8,128)} %bitcast.5, s32[128,256]{1,0:T(8,128)} %class_hbm.1, f32[3,16]{1,0:T(4,128)} %coeff_hbm.1, f32[5,128,128]{2,1,0:T(8,128)} %lag_hbm.1), custom_call_target="tpu_custom_call" | custom-call | tf_op jit(solution)/shard_map/pallas_call | solution.py:453
  25.1 1.0 %copy.8 = f32[8,128,256]{2,1,0:T(8,128)} copy(f32[8,128,256]{2,1,0:T(8,128)S(1)} %shard_map.64) | data formatting | bytes 2097152

commit v2 on v1

--- a/solution.py
+++ b/solution.py
@@ -13,8 +13,7 @@
 NTILE = 32
 NYEAR = 4
 NCLASS = 16
-GROUPS = ((0, 16), (16, 16))
-FAR_PARTS = ((0, 32),)
+GROUPS = ((0, 32),)
 MOST = 32
 LAGS = 5
 HALO = 2
@@ -316,6 +315,9 @@
 
     coefficients(class_t[...], slice(PAD, PAD + LON_DEV))
 
+    def section(f):
+        pl.when(me < NTILE)(f)
+
     forwarded = []
     edge_copies = [
         pltpu.make_async_remote_copy(
@@ -348,21 +350,27 @@
         copy.start()
         forwarded.append(copy)
         days = [day_of(d) for d in range(DAY_DEV)]
-        scatter_edges(
-            recv_own, GROUPS[group], DAY_DEV, day_of, edge_lhs, edge_rhs, edges, HALO
-        )
+
+        @section
+        def _():
+            scatter_edges(
+                recv_own, GROUPS[group], DAY_DEV, day_of, edge_lhs, edge_rhs, edges, HALO
+            )
+
         if group == len(GROUPS) - 1:
             for copy in edge_copies:
                 copy.start()
-        scatter(recv_own, GROUPS[group], days, lhs_ref, rhs_ref, field, HALO)
-
-    def halo(part):
-        senders = FAR_PARTS[part]
-        for group, (start, _) in enumerate(GROUPS):
-            if senders[0] <= start < sum(senders):
-                forwarded[group].wait_recv()
+
+        @section
+        def _():
+            scatter(recv_own, GROUPS[group], days, lhs_ref, rhs_ref, field, HALO)
+            if group == len(GROUPS) - 1:
+                for i, e in enumerate((HALO + DAY_DEV - 1, HALO + DAY_DEV - 2)):
+                    near_out[i] = smooth(e)
+
+    def scatter_far():
         days = [day_of(d + DAY_DEV - HALO) for d in range(HALO)]
-        scatter(recv_far, senders, days, lhs_ref, rhs_ref, field, 0)
+        scatter(recv_far, (0, NTILE), days, lhs_ref, rhs_ref, field, 0)
 
     def stencil(src, at, rows):
         v = src[at + (rows,)]
@@ -413,24 +421,28 @@
         own(group)
     near_copies = []
     for i, e in enumerate((HALO + DAY_DEV - 1, HALO + DAY_DEV - 2)):
-        near_out[i] = smooth(e)
         copy = pltpu.make_async_remote_copy(
             near_out.at[i], near_in.at[i], near_send.at[i], near_recv.at[i], device_id={"year": near}
         )
         copy.start()
         near_copies.append(copy)
-    for d in range(DAY_DEV - 2):
-        smooth(HALO + d)
-    mix(1)
-    mix(2)
-    for i, copy in enumerate(near_copies):
+
+    for copy in forwarded:
+        copy.wait_recv()
+
+    @section
+    def _():
+        scatter_far()
+        for d in range(DAY_DEV - 2):
+            smooth(HALO + d)
+        mix(1)
+        mix(2)
+
+    for copy in near_copies + edge_copies:
         copy.wait()
+    for i in range(HALO):
         keep(HALO + DAY_DEV + i, near_in[i])
     mix(3)
-    for part in range(len(FAR_PARTS)):
-        halo(part)
-    for copy in edge_copies:
-        copy.wait()
     smooth(1)
     smooth(0)
     mix(0)

time: 26.2 us -> 23.1 us (0.88)
  Pallas kernels: 25.1 us -> 22 us
    pallas_call x1, Pallas kernels: 25.1 us -> 22 us  [body(): pl.pallas_call(kernel, out_shape=pltpu.VMEM((DAY_DEV, LAT, LON_DEV), F32)...]
where the time goes in v2:
time: 23.1 us; the launch traced here: 22.9 us
  Pallas kernels  22 us (95%)
  local copies, waits for them, and re-layouts  0.97 us (4%)
    pallas_call x1, Pallas kernels, body(): pl.pallas_call(kernel, out_shape=pltpu.VMEM((DAY_DEV, LAT, LON_DEV), F32)...  22 us
    unnamed x1, local copies, waits for them, and re-layouts  0.97 us

profile of v2, /device:TPU:1, one launch (start us, length us, event | category | flops | bytes accessed | tf_op | source)
XLA Modules:
  0.0 22.9 jit_solution(2125702014237829601)
XLA Ops:
  0.0 22.0 %shard_map.64 = f32[8,128,256]{2,1,0:T(8,128)S(1)} custom-call(s32[8,128]{1,0:T(8,128)} %bitcast.3, s32[8,128]{1,0:T(8,128)} %bitcast.4, f32[8,128]{1,0:T(8,128)} %bitcast.5, s32[128,256]{1,0:T(8,128)} %class_hbm.1, f32[3,16]{1,0:T(4,128)} %coeff_hbm.1, f32[5,128,128]{2,1,0:T(8,128)} %lag_hbm.1), custom_call_target="tpu_custom_call" | custom-call | tf_op jit(solution)/shard_map/pallas_call | solution.py:465
  22.0 1.0 %copy.8 = f32[8,128,256]{2,1,0:T(8,128)} copy(f32[8,128,256]{2,1,0:T(8,128)S(1)} %shard_map.64) | data formatting | bytes 2097152

commit v3 on v2

--- a/solution.py
+++ b/solution.py
@@ -21,6 +21,7 @@
 PAD = 8
 F32 = jnp.float32
 BF16 = jnp.bfloat16
+F8 = jnp.float8_e4m3fn
 
 
 def dot_nt(a, b):
@@ -114,25 +115,32 @@
 
 def scatter(recv_ref, senders, days, lhs_ref, rhs_ref, field, first):
     hi, lo, cell = entries(recv_ref, senders, 1)
-    hi, lo = dense(hi), dense(lo)
+    largest = jnp.maximum(jnp.max(jnp.abs(hi + lo), axis=(0, 1), keepdims=True), 1e-35)
+    rest = (hi + lo) * (256.0 / largest)
+    pieces = []
+    for _ in range(3):
+        piece = rest.astype(F8).astype(F32)
+        rest = (rest - piece) * 16.0
+        pieces.append(dense(piece))
     col = dense(jnp.bitwise_and(cell, 255))
     plane = dense(jnp.right_shift(cell, 8))
     depth = len(col) * LANES
     column, latitude = numbers(LON_DEV), numbers(LAT)
     for k in range(len(col)):
         lanes = slice(k * LANES, (k + 1) * LANES)
-        lhs_ref[:LON_DEV, lanes] = pick(col[k], column, hi[k])
-        lhs_ref[LON_DEV:, lanes] = pick(col[k], column, lo[k])
+        for q, piece in enumerate(pieces):
+            lhs_ref[q * LON_DEV : (q + 1) * LON_DEV, lanes] = pick(col[k], column, piece[k]).astype(F8)
     for i, d in enumerate(days):
         for k in range(len(col)):
             rhs_ref[i * LAT : (i + 1) * LAT, k * LANES : (k + 1) * LANES] = pick(
                 plane[k] - d * LAT, latitude
-            )
+            ).astype(F8)
     for pair in range(len(days) // 2):
         both = dot_nt(
             lhs_ref[:, :depth], rhs_ref[2 * LAT * pair : 2 * LAT * (pair + 1), :depth]
         )
-        both = both[:LON_DEV] + both[LON_DEV:]
+        small = both[LON_DEV : 2 * LON_DEV] + both[2 * LON_DEV :] * (1.0 / 16.0)
+        both = (both[:LON_DEV] + small * (1.0 / 16.0)) * (largest * (1.0 / 256.0))
         for i in range(2):
             part = both[:, i * LAT : (i + 1) * LAT]
             e = first + 2 * pair + i
@@ -482,8 +490,8 @@
             pltpu.VMEM((LON_DEV, LAT), jnp.int32),
             pltpu.VMEM((2, PAD, LAT), jnp.int32),
             pltpu.VMEM((4, LON_DEV + 2 * PAD, LAT), F32),
-            pltpu.VMEM((2 * LON_DEV, MOST * CAP), BF16),
-            pltpu.VMEM((DAY_DEV * LAT, MOST * CAP), BF16),
+            pltpu.VMEM((3 * LON_DEV, MOST * CAP), F8),
+            pltpu.VMEM((DAY_DEV * LAT, MOST * CAP), F8),
             pltpu.VMEM((8 * DAY_DEV, 2 * MOST * CAP), BF16),
             pltpu.VMEM((LAT, 2 * MOST * CAP), BF16),
             pltpu.VMEM((DAYS_EXT, LON_DEV + 2 * PAD, LAT), F32),

time: 23.1 us -> 22.2 us (0.961)
  Pallas kernels: 22 us -> 21.1 us
    pallas_call x1, Pallas kernels: 22 us -> 21.1 us  [body(): pl.pallas_call(kernel, out_shape=pltpu.VMEM((DAY_DEV, LAT, LON_DEV), F32)...]
where the time goes in v3:
time: 22.2 us; the launch traced here: 22.1 us
  Pallas kernels  21.1 us (95%)
  local copies, waits for them, and re-layouts  0.97 us (4%)
    pallas_call x1, Pallas kernels, body(): pl.pallas_call(kernel, out_shape=pltpu.VMEM((DAY_DEV, LAT, LON_DEV), F32)...  21.1 us
    unnamed x1, local copies, waits for them, and re-layouts  0.97 us

profile of v3, /device:TPU:1, one launch (start us, length us, event | category | flops | bytes accessed | tf_op | source)
XLA Modules:
  0.0 22.1 jit_solution(15912247825994116033)
XLA Ops:
  0.0 21.1 %shard_map.64 = f32[8,128,256]{2,1,0:T(8,128)S(1)} custom-call(s32[8,128]{1,0:T(8,128)} %bitcast.3, s32[8,128]{1,0:T(8,128)} %bitcast.4, f32[8,128]{1,0:T(8,128)} %bitcast.5, s32[128,256]{1,0:T(8,128)} %class_hbm.1, f32[3,16]{1,0:T(4,128)} %coeff_hbm.1, f32[5,128,128]{2,1,0:T(8,128)} %lag_hbm.1), custom_call_target="tpu_custom_call" | custom-call | tf_op jit(solution)/shard_map/pallas_call | solution.py:473
  21.1 1.0 %copy.8 = f32[8,128,256]{2,1,0:T(8,128)} copy(f32[8,128,256]{2,1,0:T(8,128)S(1)} %shard_map.64) | data formatting | bytes 2097152

commit v4 on v3

--- a/solution.py
+++ b/solution.py
@@ -113,15 +113,24 @@
     return hi, lo, cell.astype(jnp.int32)
 
 
-def scatter(recv_ref, senders, days, lhs_ref, rhs_ref, field, first):
-    hi, lo, cell = entries(recv_ref, senders, 1)
-    largest = jnp.maximum(jnp.max(jnp.abs(hi + lo), axis=(0, 1), keepdims=True), 1e-35)
-    rest = (hi + lo) * (256.0 / largest)
+def size_of(value):
+    return jnp.maximum(jnp.max(jnp.abs(value), axis=(0, 1), keepdims=True), 1e-35)
+
+
+def eighths(value, largest):
+    rest = value * (256.0 / largest)
     pieces = []
     for _ in range(3):
         piece = rest.astype(F8).astype(F32)
         rest = (rest - piece) * 16.0
         pieces.append(dense(piece))
+    return pieces
+
+
+def scatter(recv_ref, senders, days, lhs_ref, rhs_ref, field, first):
+    hi, lo, cell = entries(recv_ref, senders, 1)
+    largest = size_of(hi + lo)
+    pieces = eighths(hi + lo, largest)
     col = dense(jnp.bitwise_and(cell, 255))
     plane = dense(jnp.right_shift(cell, 8))
     depth = len(col) * LANES
@@ -152,27 +161,30 @@
 
 def scatter_edges(recv_ref, senders, count, number_of, lhs_ref, rhs_ref, edges, first):
     rows = 4 * count
-    padded = max(rows, 16)
-    latitude, number = numbers(LAT), numbers(padded)
+    latitude, number = numbers(LAT), numbers(rows)
     blocks = 3 * senders[1] // 4
-    for j, which in enumerate((0, 2)):
-        hi, lo, cell = entries(recv_ref, senders, which)
+    found = [entries(recv_ref, senders, which) for which in (0, 2)]
+    largest = size_of(jnp.maximum(*(jnp.abs(hi + lo) for hi, lo, _ in found)))
+    for j, (hi, lo, cell) in enumerate(found):
         col = jnp.bitwise_and(cell, 255)
-        near = col >= LON_DEV - 2 if which == 0 else col < 2
+        near = col >= LON_DEV - 2 if j == 0 else col < 2
         place = 4 * number_of(jnp.right_shift(cell, 15)) + (
-            col - (LON_DEV - 2) if which == 0 else col + 2
+            col - (LON_DEV - 2) if j == 0 else col + 2
         )
         place = dense(jnp.where(near, place, -1))
         lat = dense(jnp.bitwise_and(jnp.right_shift(cell, 8), LAT - 1))
-        hi, lo = dense(hi), dense(lo)
+        pieces = eighths(hi + lo, largest)
         for k in range(blocks):
             lanes = slice((blocks * j + k) * LANES, (blocks * j + k + 1) * LANES)
-            lhs_ref[:padded, lanes] = pick(place[k], number, hi[k])
-            lhs_ref[padded : 2 * padded, lanes] = pick(place[k], number, lo[k])
-            rhs_ref[:, lanes] = pick(lat[k], latitude)
+            for q, piece in enumerate(pieces):
+                lhs_ref[q * rows : (q + 1) * rows, lanes] = pick(
+                    place[k], number, piece[k]
+                ).astype(F8)
+            rhs_ref[:, lanes] = pick(lat[k], latitude).astype(F8)
     depth = 2 * blocks * LANES
-    both = dot_nt(lhs_ref[: 2 * padded, :depth], rhs_ref[:, :depth])
-    both = both[:padded] + both[padded:]
+    both = dot_nt(lhs_ref[:, :depth], rhs_ref[:, :depth])
+    small = both[rows : 2 * rows] + both[2 * rows :] * (1.0 / 16.0)
+    both = (both[:rows] + small * (1.0 / 16.0)) * (largest * (1.0 / 256.0))
     for i in range(count):
         if senders[0] == 0:
             edges[first + i] = both[4 * i : 4 * i + 4]
@@ -437,6 +449,8 @@
 
     for copy in forwarded:
         copy.wait_recv()
+    for copy in edge_copies:
+        copy.wait()
 
     @section
     def _():
@@ -445,15 +459,15 @@
             smooth(HALO + d)
         mix(1)
         mix(2)
-
-    for copy in near_copies + edge_copies:
+        smooth(1)
+        smooth(0)
+        mix(0)
+
+    for copy in near_copies:
         copy.wait()
     for i in range(HALO):
         keep(HALO + DAY_DEV + i, near_in[i])
     mix(3)
-    smooth(1)
-    smooth(0)
-    mix(0)
 
     pltpu.make_async_remote_copy(
         recv_own.at[pl.ds(1, NTILE - 1)],
@@ -492,8 +506,8 @@
             pltpu.VMEM((4, LON_DEV + 2 * PAD, LAT), F32),
             pltpu.VMEM((3 * LON_DEV, MOST * CAP), F8),
             pltpu.VMEM((DAY_DEV * LAT, MOST * CAP), F8),
-            pltpu.VMEM((8 * DAY_DEV, 2 * MOST * CAP), BF16),
-            pltpu.VMEM((LAT, 2 * MOST * CAP), BF16),
+            pltpu.VMEM((12 * DAY_DEV, 2 * MOST * CAP), F8),
+            pltpu.VMEM((LAT, 2 * MOST * CAP), F8),
             pltpu.VMEM((DAYS_EXT, LON_DEV + 2 * PAD, LAT), F32),
             pltpu.VMEM((DAYS_EXT, 4, LAT), F32),
             pltpu.VMEM((LON_DEV + 2 * PAD, LAT), F32),

time: 22.2 us -> 21.9 us (0.986)
  Pallas kernels: 21.1 us -> 20.7 us
    pallas_call x1, Pallas kernels: 21.1 us -> 20.7 us  [body(): pl.pallas_call(kernel, out_shape=pltpu.VMEM((DAY_DEV, LAT, LON_DEV), F32)...]
where the time goes in v4:
time: 21.9 us; the launch traced here: 21.7 us
  Pallas kernels  20.7 us (95%)
  local copies, waits for them, and re-layouts  0.97 us (4%)
    pallas_call x1, Pallas kernels, body(): pl.pallas_call(kernel, out_shape=pltpu.VMEM((DAY_DEV, LAT, LON_DEV), F32)...  20.7 us
    unnamed x1, local copies, waits for them, and re-layouts  0.97 us

profile of v4, /device:TPU:1, one launch (start us, length us, event | category | flops | bytes accessed | tf_op | source)
XLA Modules:
  0.0 21.7 jit_solution(1320518814940983263)
XLA Ops:
  0.0 20.7 %shard_map.64 = f32[8,128,256]{2,1,0:T(8,128)S(1)} custom-call(s32[8,128]{1,0:T(8,128)} %bitcast.3, s32[8,128]{1,0:T(8,128)} %bitcast.4, f32[8,128]{1,0:T(8,128)} %bitcast.5, s32[128,256]{1,0:T(8,128)} %class_hbm.1, f32[3,16]{1,0:T(4,128)} %coeff_hbm.1, f32[5,128,128]{2,1,0:T(8,128)} %lag_hbm.1), custom_call_target="tpu_custom_call" | custom-call | tf_op jit(solution)/shard_map/pallas_call | solution.py:487
  20.7 1.0 %copy.8 = f32[8,128,256]{2,1,0:T(8,128)} copy(f32[8,128,256]{2,1,0:T(8,128)S(1)} %shard_map.64) | data formatting | bytes 2097152

commit v5 on v4

--- a/solution.py
+++ b/solution.py
@@ -200,6 +200,9 @@
     coeff_hbm,
     lag_hbm,
     out_ref,
+    mix_ref,
+    smooth_hi,
+    smooth_lo,
     tile_ref,
     cell_ref,
     value_ref,
@@ -221,9 +224,6 @@
     field,
     edges,
     once,
-    mix_ref,
-    smooth_hi,
-    smooth_lo,
     near_out,
     near_in,
     load_sem,
@@ -424,14 +424,9 @@
         return twice
 
     def mix(pair):
-        window = range(2 * pair, 2 * pair + LAGS + 1)
-        hi = jnp.concatenate([smooth_hi[e] for e in window], axis=1)
-        lo = jnp.concatenate([smooth_lo[e] for e in window], axis=1)
-        first = dot_nt(mix_ref[...], hi)
-        second = dot_nt(mix_ref[: 2 * LAT], lo)
-        mixed = first[: 2 * LAT] + (first[2 * LAT :] + second)
-        out_ref[day_of(2 * pair)] = mixed[:LAT]
-        out_ref[day_of(2 * pair + 1)] = mixed[LAT:]
+        mixed = mix_days(pair, mix_ref, smooth_hi, smooth_lo)
+        out_ref[2 * pair] = mixed[:LAT]
+        out_ref[2 * pair + 1] = mixed[LAT:]
 
     for copy in class_copies:
         copy.wait()
@@ -467,7 +462,6 @@
         copy.wait()
     for i in range(HALO):
         keep(HALO + DAY_DEV + i, near_in[i])
-    mix(3)
 
     pltpu.make_async_remote_copy(
         recv_own.at[pl.ds(1, NTILE - 1)],
@@ -480,15 +474,48 @@
         copy.wait_send()
 
 
+def mix_days(pair, mix_ref, smooth_hi, smooth_lo):
+    window = range(2 * pair, 2 * pair + LAGS + 1)
+    hi = jnp.concatenate([smooth_hi[e] for e in window], axis=1)
+    lo = jnp.concatenate([smooth_lo[e] for e in window], axis=1)
+    first = dot_nt(mix_ref[...], hi)
+    second = dot_nt(mix_ref[: 2 * LAT], lo)
+    return first[: 2 * LAT] + (first[2 * LAT :] + second)
+
+
+def write_out(days_ref, mix_ref, smooth_hi, smooth_lo, out_ref, last, sems):
+    odd = lax.rem(lax.axis_index("year"), 2)
+
+    def to_day(source, d):
+        copy = pltpu.make_async_copy(
+            source, out_ref.at[d + odd * (DAY_DEV - 1 - 2 * d)], sems.at[d]
+        )
+        copy.start()
+        return copy
+
+    copies = [to_day(days_ref.at[d], d) for d in range(DAY_DEV - 2)]
+    mixed = mix_days(DAY_DEV // 2 - 1, mix_ref, smooth_hi, smooth_lo)
+    for i in range(2):
+        last[i] = mixed[i * LAT : (i + 1) * LAT]
+    copies += [to_day(last.at[i], DAY_DEV - 2 + i) for i in range(2)]
+    for copy in copies:
+        copy.wait()
+
+
 def body(station_tile, station_cell, station_value, class_ids, coeff_table, lag_blocks):
     hbm = pl.BlockSpec(memory_space=pltpu.HBM)
     dma = pltpu.SemaphoreType.DMA
     groups = len(GROUPS)
-    return pl.pallas_call(
+    parts = pl.pallas_call(
         kernel,
-        out_shape=pltpu.VMEM((DAY_DEV, LAT, LON_DEV), F32),
+        out_shape=[
+            pltpu.VMEM((DAY_DEV - 2, LAT, LON_DEV), F32),
+            pltpu.VMEM((4 * LAT, (LAGS + 1) * LAT), BF16),
+            pltpu.VMEM((DAYS_EXT, LON_DEV, LAT), BF16),
+            pltpu.VMEM((DAYS_EXT, LON_DEV, LAT), BF16),
+        ],
         in_specs=[hbm] * 6,
-        out_specs=pl.BlockSpec(memory_space=pltpu.VMEM),
+        out_specs=[pl.BlockSpec(memory_space=pltpu.VMEM)] * 4,
         scratch_shapes=[
             pltpu.VMEM((8, LANES), jnp.int32),
             pltpu.VMEM((8, LANES), jnp.int32),
@@ -511,9 +538,6 @@
             pltpu.VMEM((DAYS_EXT, LON_DEV + 2 * PAD, LAT), F32),
             pltpu.VMEM((DAYS_EXT, 4, LAT), F32),
             pltpu.VMEM((LON_DEV + 2 * PAD, LAT), F32),
-            pltpu.VMEM((4 * LAT, (LAGS + 1) * LAT), BF16),
-            pltpu.VMEM((DAYS_EXT, LON_DEV, LAT), BF16),
-            pltpu.VMEM((DAYS_EXT, LON_DEV, LAT), BF16),
             pltpu.VMEM((HALO, LON_DEV, LAT), F32),
             pltpu.VMEM((HALO, LON_DEV, LAT), F32),
             dma((6,)),
@@ -544,6 +568,13 @@
             )
         )
     )
+    return pl.pallas_call(
+        write_out,
+        out_shape=jax.ShapeDtypeStruct((DAY_DEV, LAT, LON_DEV), F32),
+        in_specs=[pl.BlockSpec(memory_space=pltpu.VMEM)] * 4,
+        out_specs=pl.BlockSpec(memory_space=pl.ANY),
+        scratch_shapes=[pltpu.VMEM((2, LAT, LON_DEV), F32), dma((DAY_DEV,))],
+    )(*(pltpu.with_memory_space_constraint(x, pltpu.VMEM) for x in parts))
 
 
 def solution(mesh):

time: 21.9 us -> 21.8 us (level)
  local copies, waits for them, and re-layouts: 0.97 us -> 0 us
  Pallas kernels: 20.7 us -> 21.6 us
    unnamed x1 -> x0, local copies, waits for them, and re-layouts: 0.97 us -> none
    pallas_call x1 -> x2, Pallas kernels: 20.7 us -> 21.6 us  [the longest x1 20.2 us: body(): pl.pallas_call(kernel, out_shape=[pltpu.VMEM((DAY_DEV - 2, LAT, LON_DEV),...]
where the time goes in v5:
time: 21.8 us; the launch traced here: 21.6 us
  Pallas kernels  21.6 us (99%)
    pallas_call x1, Pallas kernels, body(): pl.pallas_call(kernel, out_shape=[pltpu.VMEM((DAY_DEV - 2, LAT, LON_DEV),...  20.2 us
    pallas_call x1, Pallas kernels, body(): pl.pallas_call(write_out, out_shape=jax.ShapeDtypeStruct((DAY_DEV, LAT, L...  1.39 us

profile of v5, /device:TPU:1, one launch (start us, length us, event | category | flops | bytes accessed | tf_op | source)
XLA Modules:
  0.0 21.6 jit_solution(13564323526518655895)
XLA Ops:
  0.0 20.2 %shard_map.64 = (f32[6,128,256]{2,1,0:T(8,128)S(1)}, bf16[512,768]{1,0:T(8,128)(2,1)S(1)}, bf16[12,256,128]{2,1,0:T(8,128)(2,1)S(1)}, bf16[12,256,128]{2,1,0:T(8,128)(2,1)S(1)}) custom-call(s32[8,128]{1,0:T(8,128)} %bitcast.3, s32[8,128]{1,0:T(8,128)} %bitcast.4, f32[8,128]{1,0:T(8,128)} %bitcast.5, s32[128,256]{1,0:T(8,128)} %class_hbm.1, ...), custom_call_target="tpu_custom_call" | custom-call | tf_op jit(solution)/shard_map/pallas_call | solution.py:509
  20.2 1.4 %shard_map.65 = f32[8,128,256]{2,1,0:T(8,128)} custom-call(f32[6,128,256]{2,1,0:T(8,128)S(1)} %get-tuple-element.9.days_ref, bf16[512,768]{1,0:T(8,128)(2,1)S(1)} %get-tuple-element.10.mix_ref, bf16[12,256,128]{2,1,0:T(8,128)(2,1)S(1)} %get-tuple-element.11.smooth_hi, bf16[12,256,128]{2,1,0:T(8,128)(2,1)S(1)} %get-tuple-element.12.smooth_lo), custom_call_target="tpu_custom_call" | custom-call | tf_op jit(solution)/shard_map/pallas_call | solution.py:571
